TPU v7x, 32 devices: a whole 2x2x4 slice. The times are simulated.
32 devices in a mesh: grp: 1, row: 1, fs: 32 (over z, y, x, core).
Axes of the slice: x: 2, y: 2, z: 4, core: 2. Of those that a mesh axis runs over, the one named last changes fastest.
Arguments:
- traces: bfloat16 [128, 512, 1024], P(('row', 'fs')), may hold values from -6 to 6
- freq_bins: int32 [4], P('grp'), may hold values from 1 to 255
- obliquity: float32 [4, 8192], P('grp'), may hold values from 0.5 to 2
- pattern: int32 [1, 8], replicated, may hold values from 0 to 63, as said below
- block_mask: int32 [1, 8], replicated, may hold values 0 or 1
- shot_bins: int32 [1, 128], replicated, may hold values from 0 to 127, each once within a row
- wavefield: bfloat16 [8192, 2, 4096], P('row', None, ('grp', 'fs')), may hold values from -0.1875 to 0.1875
Outputs:
- multiples: bfloat16 [128, 2, 4096], P('row', None, ('grp', 'fs'))
Inputs may be any that keep to these rules, and one draw needn't show every extreme that they name: `pattern`: the 8 entries of a row name different receiver patches. `shot_bins`: each row is a permutation of 0 to 127.
All inputs are finite; a program needn't handle non-finite values.
Results may differ from a plain program's by a relative error of at most 0.0058.
Values may be sent and summed in bfloat16 or wider, within the bound.
A program may use at most 128 MiB of HBM per device.

v0:
```python
import math

import jax
import jax.numpy as jnp
from jax import lax
from jax.sharding import PartitionSpec as P


def dft_rows(freq_bins, samples):
    sample_ids = jnp.arange(samples, dtype=jnp.int32)
    wrapped = freq_bins[:, None] * sample_ids[None, :] % samples
    angles = wrapped.astype(jnp.float32) * (2.0 * math.pi / samples)
    stacked = jnp.stack([jnp.cos(angles), -jnp.sin(angles)], axis=1)
    count = freq_bins.shape[0]
    return (stacked.reshape(2 * count, samples) * (1.0 / math.sqrt(samples))).astype(jnp.bfloat16)


def block_product(rows, patterns, fields, base, span, patch):
    npatches = patterns.shape[0]
    channels = rows.shape[2]
    offsets = jnp.arange(patch, dtype=jnp.int32)
    local_points = (patterns[:, :, None] * patch + offsets[None, None, :]).reshape(
        npatches, channels
    ) - base
    validity = (local_points >= 0) & (local_points < span)
    clamped = jnp.clip(local_points, 0, span - 1)
    chosen = fields[clamped]
    chosen = jnp.where(validity[:, :, None, None], chosen, jnp.zeros_like(chosen))
    real_part = chosen[:, :, 0, :]
    imag_part = chosen[:, :, 1, :]
    upper = jnp.concatenate([real_part, imag_part], axis=2)
    lower = jnp.concatenate([-imag_part, real_part], axis=2)
    stacked = jnp.concatenate([upper, lower], axis=1)
    operand = rows.reshape(npatches, patch, 2 * channels)
    result = jnp.einsum("npc,ncq->npq", operand, stacked, preferred_element_type=jnp.float32)
    return result.reshape(npatches * patch, result.shape[2])


def on_device(traces, freq_bins, obliquity, pattern, block_mask, shot_bins, wavefield):
    shots_dev, samples, channels = traces.shape
    nfreq = freq_bins.shape[0]
    patch = shot_bins.shape[1]
    fs_count = lax.axis_size("fs")
    groups = fs_count // nfreq
    row_index = lax.axis_index("row")
    fs_index = lax.axis_index("fs")
    half_rows = shots_dev * fs_count
    half_patches = half_rows // patch
    dft_table = dft_rows(freq_bins, samples)
    spectra = jnp.einsum("ft,stc->sfc", dft_table, traces, preferred_element_type=jnp.float32)
    first_shot = (row_index * fs_count + fs_index) * shots_dev
    patch_ids = (first_shot + jnp.arange(shots_dev, dtype=jnp.int32)) // patch
    offsets = jnp.arange(patch, dtype=jnp.int32)
    point_ids = (pattern[patch_ids][:, :, None] * patch + offsets[None, None, :]).reshape(
        shots_dev, channels
    )
    obl_weight = jnp.transpose(obliquity[:, point_ids], (1, 0, 2))
    live_mask = jnp.repeat(block_mask[patch_ids], patch, axis=1).astype(jnp.float32)
    scaled = (
        spectra.reshape(shots_dev, nfreq, 2, channels)
        * obl_weight[:, :, None, :]
        * live_mask[:, None, None, :]
    )
    weighted = scaled.astype(jnp.bfloat16)
    whole = lax.all_gather(weighted, "fs", axis=0, tiled=True)
    mine = lax.dynamic_index_in_dim(whole, fs_index // groups, 1, keepdims=False)
    local_bins = lax.dynamic_slice_in_dim(shot_bins, row_index * half_patches, half_patches, 0)
    shot_order = (jnp.arange(half_patches, dtype=jnp.int32)[:, None] * patch + local_bins).reshape(
        half_rows
    )
    mine = mine[shot_order]
    fields = lax.all_gather(wavefield, "row", axis=0, tiled=True)
    local_patterns = lax.dynamic_slice_in_dim(pattern, row_index * half_patches, half_patches, 0)
    product = block_product(mine, local_patterns, fields, 0, fields.shape[0], patch)
    columns = wavefield.shape[2]
    return product.reshape(half_rows, 2, columns).astype(jnp.bfloat16)


def solution(mesh):
    in_specs = (
        P(("row", "fs"), None, None),
        P("grp"),
        P("grp", None),
        P(),
        P(),
        P(),
        P("row", None, ("grp", "fs")),
    )
    out_specs = P("row", None, ("grp", "fs"))
    return jax.shard_map(
        on_device, mesh=mesh, in_specs=in_specs, out_specs=out_specs, check_vma=False
    )
```

profile of v0, /device:TPU:1, one launch (start us, length us, event | category | flops | bytes accessed | tf_op | source)
XLA Modules:
  0.0 101.1 jit_solution(6633256090440693059)
XLA Ops:
  6.5 0.0 all-gather.2.cloned.1.call-start
  6.5 0.7 multiply_bitcast_fusion
  7.2 0.1 add.171
  7.3 3.4 %copy.55 = f32[4,8192]{0,1:T(8,128)} copy(f32[4,8192]{1,0:T(4,128)} %param.9) | data formatting | bytes 262144 | tf_op args[2]
  10.8 0.0 copy-start
  10.8 13.0 %gather_fusion = f32[4096,4]{1,0:T(8,128)S(1)} fusion(f32[4,8192]{0,1:T(8,128)} %copy.55, s32[4096]{0:T(1024)S(1)} %bitcast_clamp_fusion), kind=kCustom, calls=%fused_computation | custom fusion | bytes 147456 | tf_op jit(solution)/shard_map/gather | solution.py:57
  23.7 0.6 copy.56
  24.3 0.0 copy-done
  24.3 0.2 fusion.8
  24.6 0.0 copy-start.1
  24.6 2.8 %convolution_bitcast_fusion = f32[4,8,1024]{2,1,0:T(8,128)S(1)} fusion(bf16[8,512,1]{1,0,2:T(8,128)(2,1)S(1)} %reshape.409, bf16[4,512,1024]{2,1,0:T(8,128)(2,1)} %param.7), kind=kOutput, calls=%fused_computation.3 | convolution fusion | flops 33554432 | bytes 4333568 | tf_op jit(solution)/shard_map/ft,stc->sfc/dot_general | solution.py:50
  27.4 0.1 reshape.375
  27.5 0.0 copy-done.1
  27.5 0.1 broadcast_bitcast_fusion
  27.6 0.7 fusion.1
  28.3 0.0 all-gather.2.cloned.1.call-update
  28.3 0.1 compare_select_fusion.1
  28.4 5.9 %gather_fusion.2 = bf16[1024,2,128]{2,1,0:T(2,128)(2,1)S(1)} fusion(bf16[8192,2,128]{2,1,0:T(2,128)(2,1)} %param.13, s32[1024]{0:T(1024)S(1)} %broadcast_clamp_fusion), kind=kCustom, calls=%fused_computation.2 | custom fusion | bytes 1052672 | tf_op jit(solution)/shard_map/gather | solution.py:27
  34.3 0.1 add.182
  34.4 3.7 %broadcast_select_fusion = bf16[1,1024,2,128]{3,2,1,0:T(2,128)(2,1)S(1)} fusion(pred[1024]{0:T(1024)(128)(4,1)S(1)} %compare_and_fusion, bf16[1024,2,128]{2,1,0:T(2,128)(2,1)S(1)} %gather_fusion.2), kind=kLoop, calls=%fused_computation.6 | loop fusion | flops 262144 | bytes 1049600 | tf_op jit(solution)/shard_map/jit(_where)/select_n | solution.py:28
  38.2 0.7 fusion.11
  38.9 0.1 fusion.10
  39.0 0.0 copy-start.2
  39.0 0.1 maximum_bitcast_fusion
  39.2 0.6 copy.61
  39.8 0.0 copy-done.2
  39.8 47.5 %all-gather.2.cloned.1.call-done = bf16[128,4,2,1024]{3,1,2,0:T(4,128)(2,1)} async-done(((bf16[4,4,2,1024]{3,1,2,0:T(4,128)(2,1)}), bf16[128,4,2,1024]{3,1,2,0:T(4,128)(2,1)}) %all-gather.2.cloned.1.call-update) | async-done | bytes 2097168 | tf_op jit(solution)/shard_map/all_gather | solution.py:65
  87.4 2.7 %constant_dynamic-slice_fusion = bf16[128,1,2,1024]{3,1,2,0:T(2,128)(2,1)S(1)} fusion(bf16[128,4,2,1024]{3,1,2,0:T(4,128)(2,1)} %all-gather.2.cloned.1.call-done, s32[]{:T(128)S(6)} %select_n.100), kind=kLoop, calls=%fused_computation.39 | loop fusion | bytes 1048580 | tf_op jit(solution)/shard_map/jit(dynamic_index_in_dim)/dynamic_slice | solution.py:66
  90.1 0.3 copy.82
  90.4 0.5 copy.59
  90.9 1.6 %gather_fusion.1 = bf16[128,2,1024]{2,1,0:T(2,128)(2,1)S(1)} fusion(bf16[128,2,1024]{2,1,0:T(2,128)(2,1)S(1)} %copy.59, s32[1024]{0:T(1024)S(1)} %pad_clamp_fusion), kind=kCustom, calls=%fused_computation.1 | custom fusion | bytes 1049088 | tf_op jit(solution)/shard_map/gather | solution.py:71
  92.5 0.5 copy.60
  93.1 0.5 convolution_convert_fusion
  93.6 0.7 copy.63
  (15 shorter events, 0.1 us)
Async XLA Ops:
  6.5 80.8 %all-gather.2.cloned.1.call-start = ((), (), s32[]{:S(2)}) async-start(), calls=%async_computation | async-start | bytes 2162688 | tf_op jit(solution)/shard_map/all_gather | solution.py:65
  10.8 13.6 %copy-start = (s32[4]{0:T(128)S(1)}, s32[4]{0:T(128)}, u32[]{:S(2)}) copy-start(s32[4]{0:T(128)} %param.8) | copy-start | bytes 52
  24.6 2.9 %copy-start.1 = (s32[1,8]{1,0:T(1,128)S(1)}, s32[1,8]{1,0:T(1,128)}, u32[]{:S(2)}) copy-start(s32[1,8]{1,0:T(1,128)} %param.11) | copy-start | bytes 100
  39.0 0.8 copy-start.2
Sparse Core Ops, SparseCore 0:
  28.4 58.8 all-gather.1
where the time goes:
time: 102 us; the launch traced here: 101 us
  waiting for transfers between devices  47.5 us (47%)
  local copies, waits for them, and re-layouts  31.1 us (30%)
  between operations  13.6 us (13%)
  other arithmetic  5.59 us (5%)
  matrix products  3.33 us (3%)
    all_gather x1, waiting for transfers between devices, on_device(): whole = lax.all_gather(weighted, 'fs', axis=0, tiled=True)  47.5 us
    gather x1, local copies, waits for them, and re-layouts, on_device(): obl_weight = jnp.transpose(obliquity[:, point_ids], (1, 0, 2))  13 us
    gather x1, local copies, waits for them, and re-layouts, block_product(): chosen = fields[clamped]  5.88 us
    unnamed x11, local copies, waits for them, and re-layouts  3.87 us
    select_n x1, other arithmetic, block_product(): jnp.where(validity[:, :, None, None], chosen, jnp.zeros_like(chosen))  3.74 us
    dot_general x1, matrix products, on_device(): jnp.einsum('ft,stc->sfc', dft_table, traces, preferred_element_type=jnp.f...  2.84 us
    dynamic_slice x1, local copies, waits for them, and re-layouts, on_device(): lax.dynamic_index_in_dim(whole, fs_index // groups, 1, keepdims=False)  2.7 us
    gather x2, local copies, waits for them, and re-layouts, on_device(): mine = mine[shot_order]  2.17 us
  transfers between devices with their start and end apart: 1, of which 1 were waited for; matrix products, arithmetic and copies ran while one was open for 11% of the time, Pallas kernels for 0%

commit v1 on v0

v1 whole, which is shorter than its diff:
```python
import functools
import math

import jax
import jax.numpy as jnp
from jax import lax
from jax.experimental import pallas as pl
from jax.experimental.pallas import tpu as pltpu
from jax.sharding import PartitionSpec as P


def dot(left, right):
    return jnp.dot(left, right, preferred_element_type=jnp.float32)


def iota(shape, axis):
    return lax.broadcasted_iota(jnp.int32, shape, axis)


def dft_rows(freq_ref, nfreq, shots, samples):
    shape = (nfreq * 2 * shots, samples)
    row = iota(shape, 0)
    freq = jnp.zeros(shape, jnp.int32)
    for f in range(nfreq):
        freq = jnp.where(lax.div(row, 2 * shots) == f, freq_ref[f], freq)
    quarter = lax.rem(lax.div(row, shots), 2) * (samples // 4)
    wrapped = (freq * iota(shape, 1) + quarter) & (samples - 1)
    folded = jnp.abs(wrapped - samples // 2) - samples // 4
    angles = folded.astype(jnp.float32) * (2.0 * math.pi / samples)
    return jnp.sin(angles) * (1.0 / math.sqrt(samples))


def kernel(
    nfs,
    nfreq,
    half_patches,
    freq_ref,
    pattern_ref,
    mask_ref,
    bins_ref,
    obl_hbm,
    traces_hbm,
    field_hbm,
    out_ref,
    obl,
    traces,
    field,
    table,
    staged,
    arrived,
    gathered,
    chosen,
    order,
    load_sem,
    send1,
    recv1,
    send2,
    recv2,
):
    shots, samples, channels = traces.shape
    blocks = pattern_ref.shape[1]
    patch = channels // blocks
    group = nfs // nfreq
    pair = 2 * shots
    half = channels // 2
    rows = group * nfreq * pair
    me = lax.axis_index("fs")
    mine, member = lax.div(me, group), lax.rem(me, group)
    patch_id = lax.axis_index("row") * half_patches + lax.div(me * shots, patch)

    loads = [pltpu.make_async_copy(obl_hbm, obl, load_sem.at[0])]
    for s in range(shots):
        loads.append(
            pltpu.make_async_copy(traces_hbm.at[s], traces.at[s], load_sem.at[1 + s])
        )
    loads.append(pltpu.make_async_copy(field_hbm, field, load_sem.at[1 + shots]))
    for load in loads:
        load.start()

    def same_member(k):
        return lax.rem(mine + k, nfreq)

    def same_group(k):
        return mine * group + lax.rem(member + k, group)

    barrier = pltpu.get_barrier_semaphore()
    for k in range(1, nfreq):
        pl.semaphore_signal(
            barrier,
            inc=1,
            device_id={"fs": same_member(k) * group + member},
            device_id_type=pl.DeviceIdType.MESH,
        )
    for k in range(1, group):
        pl.semaphore_signal(
            barrier,
            inc=1,
            device_id={"fs": same_group(k)},
            device_id_type=pl.DeviceIdType.MESH,
        )

    rows_table = dft_rows(freq_ref, nfreq, shots, samples)
    owner = lax.rem(iota(rows_table.shape, 0), shots)
    for s in range(shots):
        table[:, s * samples : (s + 1) * samples] = jnp.where(
            owner == s, rows_table, 0.0
        ).astype(jnp.bfloat16)

    for a in range(half_patches):
        bins = bins_ref[pl.ds(lax.axis_index("row") * half_patches + a, 1), :]
        shot = bins + a * patch
        device = lax.div(shot, shots)
        place = (
            lax.rem(device, group) * (nfreq * pair)
            + lax.div(device, group) * pair
            + lax.rem(shot, shots)
        )
        hot = jnp.where(iota((rows, patch), 0) == place, 1.0, 0.0).astype(jnp.bfloat16)
        for j in range(2):
            spread = jnp.where(
                iota((2 * patch, patch), 0) == 2 * iota((2 * patch, patch), 1) + j, 1.0, 0.0
            ).astype(jnp.bfloat16)
            order[a, :, j * rows : (j + 1) * rows] = lax.dot_general(
                spread, hot, (((1,), (1,)), ((), ())), preferred_element_type=jnp.float32
            ).astype(jnp.bfloat16)

    loads[0].wait()
    weights = []
    for b in range(blocks):
        live = mask_ref[patch_id, b].astype(jnp.float32)
        weights.append(obl[pattern_ref[patch_id, b]] * live)
    weights = jnp.concatenate(weights, axis=1)

    spectra = jnp.zeros((nfreq * pair, channels), jnp.float32)
    for s in range(shots):
        loads[1 + s].wait()
        spectra += dot(table[:, s * samples : (s + 1) * samples], traces[s])
    for f in range(nfreq):
        scaled = spectra[f * pair : (f + 1) * pair] * weights[f : f + 1]
        staged[f] = jnp.concatenate([scaled[:, :half], scaled[:, half:]], axis=0).astype(
            jnp.bfloat16
        )
    pl.semaphore_wait(barrier, nfreq - 1 + group - 1)

    first = []
    for k in range(1, nfreq):
        copy = pltpu.make_async_remote_copy(
            src_ref=staged.at[same_member(k)],
            dst_ref=arrived.at[mine],
            send_sem=send1.at[k - 1],
            recv_sem=recv1.at[k - 1],
            device_id={"fs": same_member(k) * group + member},
            device_id_type=pl.DeviceIdType.MESH,
        )
        copy.start()
        first.append(copy)
    arrived[mine] = staged[mine]

    loads[1 + shots].wait()
    spot = iota((2 * patch, 2 * patch), 0)
    source = jnp.where(spot < patch, 2 * spot, 2 * (spot - patch) + 1)
    split = jnp.where(iota((2 * patch, 2 * patch), 1) == source, 1.0, 0.0).astype(jnp.bfloat16)
    for a in range(half_patches):
        for b in range(blocks):
            block = pattern_ref[lax.axis_index("row") * half_patches + a, b]
            parts = dot(split, field[block]).astype(jnp.bfloat16)
            width = parts.shape[1]
            chosen[a, b * patch : (b + 1) * patch, :width] = parts[:patch]
            chosen[a, b * patch : (b + 1) * patch, width:] = parts[patch:]

    for copy in first:
        copy.wait_recv()
    pieces = []
    for z in range(nfreq):
        piece = arrived[z].astype(jnp.float32)
        pieces.append(jnp.concatenate([piece[:pair], piece[pair:]], axis=1))
    gathered[member] = jnp.concatenate(pieces, axis=0).astype(jnp.bfloat16)

    second = []
    for k in range(1, group):
        copy = pltpu.make_async_remote_copy(
            src_ref=gathered.at[member],
            dst_ref=gathered.at[member],
            send_sem=send2.at[k - 1],
            recv_sem=recv2.at[k - 1],
            device_id={"fs": same_group(k)},
            device_id_type=pl.DeviceIdType.MESH,
        )
        copy.start()
        second.append(copy)
    for copy in second:
        copy.wait_recv()

    width = field.shape[2]
    left = gathered[...].reshape(rows, channels)
    for a in range(half_patches):
        product = dot(left, chosen[a])
        by_real, by_imag = product[:, :width], product[:, width:]
        real = by_real - pltpu.roll(by_imag, rows - shots, 0)
        imag = by_imag + pltpu.roll(by_real, rows - shots, 0)
        both = jnp.concatenate([real, imag], axis=0).astype(jnp.bfloat16)
        out_ref[a * 2 * patch : (a + 1) * 2 * patch, :] = dot(order[a], both).astype(
            jnp.bfloat16
        )
    for copy in first + second:
        copy.wait_send()


def on_device(traces, freq_bins, obliquity, pattern, block_mask, shot_bins, wavefield):
    shots, samples, channels = traces.shape
    nfreq = freq_bins.shape[0]
    patch = shot_bins.shape[1]
    nfs = lax.axis_size("fs")
    group = nfs // nfreq
    half_patches = shots * nfs // patch
    columns = wavefield.shape[2]
    if lax.axis_size("row") > 1:
        wavefield = lax.all_gather(wavefield, "row", axis=0, tiled=True)
    points = wavefield.shape[0]
    rows = group * nfreq * 2 * shots
    smem = pl.BlockSpec(memory_space=pltpu.SMEM)
    vmem = pl.BlockSpec(memory_space=pltpu.VMEM)
    hbm = pl.BlockSpec(memory_space=pl.ANY)
    result = pl.pallas_call(
        functools.partial(kernel, nfs, nfreq, half_patches),
        out_shape=jax.ShapeDtypeStruct((half_patches * patch * 2, columns), jnp.bfloat16),
        in_specs=[smem, smem, smem, vmem, hbm, hbm, hbm],
        out_specs=vmem,
        scratch_shapes=[
            pltpu.VMEM((points // patch, nfreq, patch), jnp.float32),
            pltpu.VMEM(traces.shape, jnp.bfloat16),
            pltpu.VMEM((points // patch, 2 * patch, columns), jnp.bfloat16),
            pltpu.VMEM((nfreq * 2 * shots, shots * samples), jnp.bfloat16),
            pltpu.VMEM((nfreq, 4 * shots, channels // 2), jnp.bfloat16),
            pltpu.VMEM((nfreq, 4 * shots, channels // 2), jnp.bfloat16),
            pltpu.VMEM((group, nfreq * 2 * shots, channels), jnp.bfloat16),
            pltpu.VMEM((half_patches, channels, 2 * columns), jnp.bfloat16),
            pltpu.VMEM((half_patches, 2 * patch, 2 * rows), jnp.bfloat16),
            pltpu.SemaphoreType.DMA((2 + shots,)),
            pltpu.SemaphoreType.DMA((nfreq - 1,)),
            pltpu.SemaphoreType.DMA((nfreq - 1,)),
            pltpu.SemaphoreType.DMA((group - 1,)),
            pltpu.SemaphoreType.DMA((group - 1,)),
        ],
        compiler_params=pltpu.CompilerParams(
            collective_id=0, has_side_effects=True, vmem_limit_bytes=60 * 1024 * 1024
        ),
    )(
        freq_bins,
        pattern,
        block_mask,
        shot_bins,
        obliquity.reshape(nfreq, points // patch, patch).transpose(1, 0, 2),
        traces,
        wavefield.reshape(points // patch, 2 * patch, columns),
    )
    return result.reshape(half_patches * patch, 2, columns)


def solution(mesh):
    in_specs = (
        P(("row", "fs"), None, None),
        P("grp"),
        P("grp", None),
        P(),
        P(),
        P(),
        P("row", None, ("grp", "fs")),
    )
    out_specs = P("row", None, ("grp", "fs"))
    return jax.shard_map(
        on_device, mesh=mesh, in_specs=in_specs, out_specs=out_specs, check_vma=False
    )
```

time: 102 us -> 19.7 us (0.19)
  waiting for transfers between devices: 47.5 us -> 0 us
  local copies, waits for them, and re-layouts: 31.1 us -> 1.52 us
  Pallas kernels: 0 us -> 18 us
  between operations: 13.6 us -> 0.01 us
  other arithmetic: 5.59 us -> 0 us
  matrix products: 3.33 us -> 0 us
    all_gather x1 -> x0, waiting for transfers between devices: 47.5 us -> none  [on_device(): whole = lax.all_gather(weighted, 'fs', axis=0, tiled=True)]
    gather x4 -> x0, local copies, waits for them, and re-layouts: 21 us -> none  [the longest x1 13 us: on_device(): obl_weight = jnp.transpose(obliquity[:, point_ids], (1, 0, 2))]
    pallas_call x0 -> x1, Pallas kernels: none -> 18 us  [on_device(): pl.pallas_call(functools.partial(kernel, nfs, nfreq, half_patches), out_s...]
    select_n x3 -> x0, other arithmetic: 3.82 us -> none  [the longest x1 3.74 us: block_product(): jnp.where(validity[:, :, None, None], chosen, jnp.zeros_like(chosen))]
    dot_general x2 -> x0, matrix products: 3.33 us -> none  [the longest x1 2.84 us: on_device(): jnp.einsum('ft,stc->sfc', dft_table, traces, preferred_element_type=jnp.f...]
    dynamic_slice x1 -> x0, local copies, waits for them, and re-layouts: 2.7 us -> none  [on_device(): lax.dynamic_index_in_dim(whole, fs_index // groups, 1, keepdims=False)]
    unnamed x11 -> x1, local copies, waits for them, and re-layouts: 3.87 us -> 1.52 us
  transfers between devices with their start and end apart: 1 -> 0, of which waited for: 1 -> 0; matrix products, arithmetic and copies ran while one was open for 11% -> 0% of each run, Pallas kernels for 0% -> 0%
where the time goes in v1:
time: 19.7 us; the launch traced here: 19.5 us
  Pallas kernels  18 us (91%)
  local copies, waits for them, and re-layouts  1.52 us (8%)
    pallas_call x1, Pallas kernels, on_device(): pl.pallas_call(functools.partial(kernel, nfs, nfreq, half_patches), out_s...  18 us
    unnamed x1, local copies, waits for them, and re-layouts  1.52 us

profile of v1, /device:TPU:1, one launch (start us, length us, event | category | flops | bytes accessed | tf_op | source)
XLA Modules:
  0.0 19.5 jit_solution(1143689286234389867)
XLA Ops:
  0.0 18.0 %shard_map.73 = bf16[256,128]{1,0:T(8,128)(2,1)} custom-call(s32[4]{0:T(128)} %freq_ref.1, s32[1,8]{1,0:T(1,128)} %pattern_ref.1, s32[1,8]{1,0:T(1,128)} %mask_ref.1, s32[1,128]{1,0:T(1,128)} %bins_ref.1, f32[64,4,128]{2,1,0:T(4,128)} %bitcast.7, bf16[4,512,1024]{2,1,0:T(8,128)(2,1)} %traces_hbm.1, bf16[64,256,128]{2,1,0:T(8,128)(2,1)} %bitcast.5), custom_call_target="tpu_custom_call" | custom-call | tf_op jit(solution)/shard_map/pallas_call | solution.py:224
  18.0 1.5 %copy.9 = bf16[128,2,128]{2,1,0:T(2,128)(2,1)} copy(bf16[128,2,128]{2,1,0:T(2,128)(2,1)} %bitcast.6) | data formatting | bytes 131072

commit v2 on v1

--- a/solution.py
+++ b/solution.py
@@ -47,23 +47,27 @@
     field,
     table,
     staged,
-    arrived,
     gathered,
     chosen,
     order,
+    product,
     load_sem,
-    send1,
-    recv1,
-    send2,
-    recv2,
+    send_z,
+    recv_z,
+    send_chip,
+    recv_chip,
+    send_core,
+    recv_core,
 ):
     shots, samples, channels = traces.shape
     blocks = pattern_ref.shape[1]
     patch = channels // blocks
     group = nfs // nfreq
+    chips = group // 2
     pair = 2 * shots
     half = channels // 2
-    rows = group * nfreq * pair
+    share = group * pair
+    rows = nfreq * share
     me = lax.axis_index("fs")
     mine, member = lax.div(me, group), lax.rem(me, group)
     patch_id = lax.axis_index("row") * half_patches + lax.div(me * shots, patch)
@@ -77,26 +81,34 @@
     for load in loads:
         load.start()
 
-    def same_member(k):
+    chip, core = lax.div(member, 2), lax.rem(member, 2)
+    sibling = member + 1 - 2 * core
+
+    def plane(k):
         return lax.rem(mine + k, nfreq)
 
-    def same_group(k):
-        return mine * group + lax.rem(member + k, group)
+    def other_chip(q):
+        return lax.rem(chip + q, chips) * 2 + core
+
+    def send(src, dst, send_sem, recv_sem, target):
+        copy = pltpu.make_async_remote_copy(
+            src_ref=src,
+            dst_ref=dst,
+            send_sem=send_sem,
+            recv_sem=recv_sem,
+            device_id={"fs": target},
+            device_id_type=pl.DeviceIdType.MESH,
+        )
+        copy.start()
+        return copy
 
     barrier = pltpu.get_barrier_semaphore()
-    for k in range(1, nfreq):
+    partners = [plane(k) * group + member for k in range(1, nfreq)]
+    partners += [mine * group + other_chip(q) for q in range(1, chips)]
+    partners += [mine * group + sibling]
+    for partner in partners:
         pl.semaphore_signal(
-            barrier,
-            inc=1,
-            device_id={"fs": same_member(k) * group + member},
-            device_id_type=pl.DeviceIdType.MESH,
-        )
-    for k in range(1, group):
-        pl.semaphore_signal(
-            barrier,
-            inc=1,
-            device_id={"fs": same_group(k)},
-            device_id_type=pl.DeviceIdType.MESH,
+            barrier, inc=1, device_id={"fs": partner}, device_id_type=pl.DeviceIdType.MESH
         )
 
     rows_table = dft_rows(freq_ref, nfreq, shots, samples)
@@ -111,17 +123,17 @@
         shot = bins + a * patch
         device = lax.div(shot, shots)
         place = (
-            lax.rem(device, group) * (nfreq * pair)
-            + lax.div(device, group) * pair
+            lax.rem(mine + nfreq - lax.div(device, group), nfreq) * share
+            + lax.rem(device, group) * pair
             + lax.rem(shot, shots)
         )
         hot = jnp.where(iota((rows, patch), 0) == place, 1.0, 0.0).astype(jnp.bfloat16)
         for j in range(2):
-            spread = jnp.where(
+            double = jnp.where(
                 iota((2 * patch, patch), 0) == 2 * iota((2 * patch, patch), 1) + j, 1.0, 0.0
             ).astype(jnp.bfloat16)
             order[a, :, j * rows : (j + 1) * rows] = lax.dot_general(
-                spread, hot, (((1,), (1,)), ((), ())), preferred_element_type=jnp.float32
+                double, hot, (((1,), (1,)), ((), ())), preferred_element_type=jnp.float32
             ).astype(jnp.bfloat16)
 
     loads[0].wait()
@@ -140,23 +152,65 @@
         staged[f] = jnp.concatenate([scaled[:, :half], scaled[:, half:]], axis=0).astype(
             jnp.bfloat16
         )
-    pl.semaphore_wait(barrier, nfreq - 1 + group - 1)
-
-    first = []
-    for k in range(1, nfreq):
-        copy = pltpu.make_async_remote_copy(
-            src_ref=staged.at[same_member(k)],
-            dst_ref=arrived.at[mine],
-            send_sem=send1.at[k - 1],
-            recv_sem=recv1.at[k - 1],
-            device_id={"fs": same_member(k) * group + member},
-            device_id_type=pl.DeviceIdType.MESH,
-        )
-        copy.start()
-        first.append(copy)
-    arrived[mine] = staged[mine]
+    pl.semaphore_wait(barrier, len(partners))
+
+    by_z = [
+        send(
+            staged.at[plane(k)],
+            gathered.at[k, member],
+            send_z.at[k - 1],
+            recv_z.at[k - 1],
+            plane(k) * group + member,
+        )
+        for k in range(1, nfreq)
+    ]
+    gathered[0, member] = staged[mine]
+    by_chip, by_core = [], []
+
+    def spread(k):
+        block = gathered.at[k, member]
+        by_chip.append(
+            [
+                send(
+                    block,
+                    block,
+                    send_chip.at[k, q - 1],
+                    recv_chip.at[k, q - 1],
+                    mine * group + other_chip(q),
+                )
+                for q in range(1, chips)
+            ]
+        )
+        by_core.append(
+            [
+                send(
+                    block,
+                    block,
+                    send_core.at[k, 0],
+                    recv_core.at[k, 0],
+                    mine * group + sibling,
+                )
+            ]
+        )
+
+    def forward(k):
+        for q in range(1, chips):
+            by_chip[k][q - 1].wait_recv()
+            block = gathered.at[k, lax.rem(chip + chips - q, chips) * 2 + core]
+            by_core[k].append(
+                send(
+                    block,
+                    block,
+                    send_core.at[k, q],
+                    recv_core.at[k, q],
+                    mine * group + sibling,
+                )
+            )
+
+    spread(0)
 
     loads[1 + shots].wait()
+    width = field.shape[2]
     spot = iota((2 * patch, 2 * patch), 0)
     source = jnp.where(spot < patch, 2 * spot, 2 * (spot - patch) + 1)
     split = jnp.where(iota((2 * patch, 2 * patch), 1) == source, 1.0, 0.0).astype(jnp.bfloat16)
@@ -164,45 +218,35 @@
         for b in range(blocks):
             block = pattern_ref[lax.axis_index("row") * half_patches + a, b]
             parts = dot(split, field[block]).astype(jnp.bfloat16)
-            width = parts.shape[1]
-            chosen[a, b * patch : (b + 1) * patch, :width] = parts[:patch]
-            chosen[a, b * patch : (b + 1) * patch, width:] = parts[patch:]
-
-    for copy in first:
-        copy.wait_recv()
-    pieces = []
-    for z in range(nfreq):
-        piece = arrived[z].astype(jnp.float32)
-        pieces.append(jnp.concatenate([piece[:pair], piece[pair:]], axis=1))
-    gathered[member] = jnp.concatenate(pieces, axis=0).astype(jnp.bfloat16)
-
-    second = []
-    for k in range(1, group):
-        copy = pltpu.make_async_remote_copy(
-            src_ref=gathered.at[member],
-            dst_ref=gathered.at[member],
-            send_sem=send2.at[k - 1],
-            recv_sem=recv2.at[k - 1],
-            device_id={"fs": same_group(k)},
-            device_id_type=pl.DeviceIdType.MESH,
-        )
-        copy.start()
-        second.append(copy)
-    for copy in second:
-        copy.wait_recv()
-
-    width = field.shape[2]
-    left = gathered[...].reshape(rows, channels)
+            top = b * patch % half
+            side = b * patch // half * 2 * width
+            chosen[a, top : top + patch, side : side + width] = parts[:patch]
+            chosen[a, top : top + patch, side + width : side + 2 * width] = parts[patch:]
+
+    for k in range(1, nfreq):
+        by_z[k - 1].wait_recv()
+        spread(k)
+    for k in range(nfreq):
+        forward(k)
+    for k in range(nfreq):
+        for copy in by_core[k]:
+            copy.wait_recv()
+        left = gathered[k].reshape(2 * share, half)
+        for a in range(half_patches):
+            halves = dot(left, chosen[a]).reshape(group, 2, pair, 4 * width)
+            total = (halves[:, 0, :, : 2 * width] + halves[:, 1, :, 2 * width :]).reshape(
+                share, 2 * width
+            )
+            by_real, by_imag = total[:, :width], total[:, width:]
+            real = by_real - pltpu.roll(by_imag, share - shots, 0)
+            imag = by_imag + pltpu.roll(by_real, share - shots, 0)
+            product[a, k * share : (k + 1) * share] = real.astype(jnp.bfloat16)
+            product[a, rows + k * share : rows + (k + 1) * share] = imag.astype(jnp.bfloat16)
     for a in range(half_patches):
-        product = dot(left, chosen[a])
-        by_real, by_imag = product[:, :width], product[:, width:]
-        real = by_real - pltpu.roll(by_imag, rows - shots, 0)
-        imag = by_imag + pltpu.roll(by_real, rows - shots, 0)
-        both = jnp.concatenate([real, imag], axis=0).astype(jnp.bfloat16)
-        out_ref[a * 2 * patch : (a + 1) * 2 * patch, :] = dot(order[a], both).astype(
+        out_ref[a * 2 * patch : (a + 1) * 2 * patch, :] = dot(order[a], product[a]).astype(
             jnp.bfloat16
         )
-    for copy in first + second:
+    for copy in by_z + sum(by_chip, []) + sum(by_core, []):
         copy.wait_send()
 
 
@@ -232,15 +276,17 @@
             pltpu.VMEM((points // patch, 2 * patch, columns), jnp.bfloat16),
             pltpu.VMEM((nfreq * 2 * shots, shots * samples), jnp.bfloat16),
             pltpu.VMEM((nfreq, 4 * shots, channels // 2), jnp.bfloat16),
-            pltpu.VMEM((nfreq, 4 * shots, channels // 2), jnp.bfloat16),
-            pltpu.VMEM((group, nfreq * 2 * shots, channels), jnp.bfloat16),
-            pltpu.VMEM((half_patches, channels, 2 * columns), jnp.bfloat16),
+            pltpu.VMEM((nfreq, group, 4 * shots, channels // 2), jnp.bfloat16),
+            pltpu.VMEM((half_patches, channels // 2, 4 * columns), jnp.bfloat16),
             pltpu.VMEM((half_patches, 2 * patch, 2 * rows), jnp.bfloat16),
+            pltpu.VMEM((half_patches, 2 * rows, columns), jnp.bfloat16),
             pltpu.SemaphoreType.DMA((2 + shots,)),
             pltpu.SemaphoreType.DMA((nfreq - 1,)),
             pltpu.SemaphoreType.DMA((nfreq - 1,)),
-            pltpu.SemaphoreType.DMA((group - 1,)),
-            pltpu.SemaphoreType.DMA((group - 1,)),
+            pltpu.SemaphoreType.DMA((nfreq, group // 2 - 1)),
+            pltpu.SemaphoreType.DMA((nfreq, group // 2 - 1)),
+            pltpu.SemaphoreType.DMA((nfreq, group // 2)),
+            pltpu.SemaphoreType.DMA((nfreq, group // 2)),
         ],
         compiler_params=pltpu.CompilerParams(
             collective_id=0, has_side_effects=True, vmem_limit_bytes=60 * 1024 * 1024

time: 19.7 us -> 19 us (0.964)
  Pallas kernels: 18 us -> 17.3 us
    pallas_call x1, Pallas kernels: 18 us -> 17.3 us  [on_device(): pl.pallas_call(functools.partial(kernel, nfs, nfreq, half_patches), out_s...]
where the time goes in v2:
time: 19 us; the launch traced here: 18.9 us
  Pallas kernels  17.3 us (91%)
  local copies, waits for them, and re-layouts  1.52 us (8%)
    pallas_call x1, Pallas kernels, on_device(): pl.pallas_call(functools.partial(kernel, nfs, nfreq, half_patches), out_s...  17.3 us
    unnamed x1, local copies, waits for them, and re-layouts  1.52 us

profile of v2, /device:TPU:1, one launch (start us, length us, event | category | flops | bytes accessed | tf_op | source)
XLA Modules:
  0.0 18.9 jit_solution(310087325858156827)
XLA Ops:
  0.0 17.3 %shard_map.73 = bf16[256,128]{1,0:T(8,128)(2,1)} custom-call(s32[4]{0:T(128)} %freq_ref.1, s32[1,8]{1,0:T(1,128)} %pattern_ref.1, s32[1,8]{1,0:T(1,128)} %mask_ref.1, s32[1,128]{1,0:T(1,128)} %bins_ref.1, f32[64,4,128]{2,1,0:T(4,128)} %bitcast.7, bf16[4,512,1024]{2,1,0:T(8,128)(2,1)} %traces_hbm.1, bf16[64,256,128]{2,1,0:T(8,128)(2,1)} %bitcast.5), custom_call_target="tpu_custom_call" | custom-call | tf_op jit(solution)/shard_map/pallas_call | solution.py:268
  17.4 1.5 %copy.9 = bf16[128,2,128]{2,1,0:T(2,128)(2,1)} copy(bf16[128,2,128]{2,1,0:T(2,128)(2,1)} %bitcast.6) | data formatting | bytes 131072

commit v3 on v2

--- a/solution.py
+++ b/solution.py
@@ -34,14 +34,18 @@
     nfs,
     nfreq,
     half_patches,
+    freq_hbm,
+    pattern_hbm,
+    mask_hbm,
+    bins_hbm,
+    obl_hbm,
+    traces_hbm,
+    field_hbm,
+    out_ref,
     freq_ref,
     pattern_ref,
     mask_ref,
     bins_ref,
-    obl_hbm,
-    traces_hbm,
-    field_hbm,
-    out_ref,
     obl,
     traces,
     field,
@@ -72,15 +76,6 @@
     mine, member = lax.div(me, group), lax.rem(me, group)
     patch_id = lax.axis_index("row") * half_patches + lax.div(me * shots, patch)
 
-    loads = [pltpu.make_async_copy(obl_hbm, obl, load_sem.at[0])]
-    for s in range(shots):
-        loads.append(
-            pltpu.make_async_copy(traces_hbm.at[s], traces.at[s], load_sem.at[1 + s])
-        )
-    loads.append(pltpu.make_async_copy(field_hbm, field, load_sem.at[1 + shots]))
-    for load in loads:
-        load.start()
-
     chip, core = lax.div(member, 2), lax.rem(member, 2)
     sibling = member + 1 - 2 * core
 
@@ -111,6 +106,20 @@
             barrier, inc=1, device_id={"fs": partner}, device_id_type=pl.DeviceIdType.MESH
         )
 
+    def load(src, dst, index):
+        copy = pltpu.make_async_copy(src, dst, load_sem.at[index])
+        copy.start()
+        return copy
+
+    get_freq = load(freq_hbm, freq_ref, 0)
+    get_traces = [load(traces_hbm.at[s], traces.at[s], 6 + s) for s in range(shots)]
+    get_pattern = load(pattern_hbm, pattern_ref, 1)
+    get_mask = load(mask_hbm, mask_ref, 2)
+    get_obl = load(obl_hbm, obl, 3)
+    get_bins = load(bins_hbm, bins_ref, 4)
+    get_field = load(field_hbm, field, 5)
+
+    get_freq.wait()
     rows_table = dft_rows(freq_ref, nfreq, shots, samples)
     owner = lax.rem(iota(rows_table.shape, 0), shots)
     for s in range(shots):
@@ -118,12 +127,15 @@
             owner == s, rows_table, 0.0
         ).astype(jnp.bfloat16)
 
+    get_bins.wait()
     for a in range(half_patches):
         bins = bins_ref[pl.ds(lax.axis_index("row") * half_patches + a, 1), :]
         shot = bins + a * patch
         device = lax.div(shot, shots)
+        source = lax.div(device, group)
+        slot = jnp.where(source < mine, source + 1, jnp.where(source == mine, 0, source))
         place = (
-            lax.rem(mine + nfreq - lax.div(device, group), nfreq) * share
+            slot * share
             + lax.rem(device, group) * pair
             + lax.rem(shot, shots)
         )
@@ -136,7 +148,9 @@
                 double, hot, (((1,), (1,)), ((), ())), preferred_element_type=jnp.float32
             ).astype(jnp.bfloat16)
 
-    loads[0].wait()
+    get_pattern.wait()
+    get_mask.wait()
+    get_obl.wait()
     weights = []
     for b in range(blocks):
         live = mask_ref[patch_id, b].astype(jnp.float32)
@@ -145,7 +159,7 @@
 
     spectra = jnp.zeros((nfreq * pair, channels), jnp.float32)
     for s in range(shots):
-        loads[1 + s].wait()
+        get_traces[s].wait()
         spectra += dot(table[:, s * samples : (s + 1) * samples], traces[s])
     for f in range(nfreq):
         scaled = spectra[f * pair : (f + 1) * pair] * weights[f : f + 1]
@@ -154,16 +168,19 @@
         )
     pl.semaphore_wait(barrier, len(partners))
 
-    by_z = [
-        send(
-            staged.at[plane(k)],
-            gathered.at[k, member],
-            send_z.at[k - 1],
-            recv_z.at[k - 1],
-            plane(k) * group + member,
-        )
-        for k in range(1, nfreq)
-    ]
+    by_z = []
+    for k in range(1, nfreq):
+        target = plane(k)
+        slot = mine + 1 - lax.div(mine + nfreq - target, nfreq)
+        by_z.append(
+            send(
+                staged.at[target],
+                gathered.at[slot, member],
+                send_z.at[k - 1],
+                recv_z.at[slot - 1],
+                target * group + member,
+            )
+        )
     gathered[0, member] = staged[mine]
     by_chip, by_core = [], []
 
@@ -209,7 +226,19 @@
 
     spread(0)
 
-    loads[1 + shots].wait()
+    for k in range(1, nfreq):
+        block = gathered.at[k, member]
+        pltpu.make_async_remote_copy(
+            src_ref=block,
+            dst_ref=block,
+            send_sem=send_z.at[k - 1],
+            recv_sem=recv_z.at[k - 1],
+            device_id={"fs": plane(k) * group + member},
+            device_id_type=pl.DeviceIdType.MESH,
+        ).wait_recv()
+        spread(k)
+
+    get_field.wait()
     width = field.shape[2]
     spot = iota((2 * patch, 2 * patch), 0)
     source = jnp.where(spot < patch, 2 * spot, 2 * (spot - patch) + 1)
@@ -223,9 +252,6 @@
             chosen[a, top : top + patch, side : side + width] = parts[:patch]
             chosen[a, top : top + patch, side + width : side + 2 * width] = parts[patch:]
 
-    for k in range(1, nfreq):
-        by_z[k - 1].wait_recv()
-        spread(k)
     for k in range(nfreq):
         forward(k)
     for k in range(nfreq):
@@ -262,15 +288,18 @@
         wavefield = lax.all_gather(wavefield, "row", axis=0, tiled=True)
     points = wavefield.shape[0]
     rows = group * nfreq * 2 * shots
-    smem = pl.BlockSpec(memory_space=pltpu.SMEM)
     vmem = pl.BlockSpec(memory_space=pltpu.VMEM)
     hbm = pl.BlockSpec(memory_space=pl.ANY)
     result = pl.pallas_call(
         functools.partial(kernel, nfs, nfreq, half_patches),
         out_shape=jax.ShapeDtypeStruct((half_patches * patch * 2, columns), jnp.bfloat16),
-        in_specs=[smem, smem, smem, vmem, hbm, hbm, hbm],
+        in_specs=[hbm] * 7,
         out_specs=vmem,
         scratch_shapes=[
+            pltpu.SMEM(freq_bins.shape, jnp.int32),
+            pltpu.SMEM(pattern.shape, jnp.int32),
+            pltpu.SMEM(block_mask.shape, jnp.int32),
+            pltpu.VMEM(shot_bins.shape, jnp.int32),
             pltpu.VMEM((points // patch, nfreq, patch), jnp.float32),
             pltpu.VMEM(traces.shape, jnp.bfloat16),
             pltpu.VMEM((points // patch, 2 * patch, columns), jnp.bfloat16),
@@ -280,7 +309,7 @@
             pltpu.VMEM((half_patches, channels // 2, 4 * columns), jnp.bfloat16),
             pltpu.VMEM((half_patches, 2 * patch, 2 * rows), jnp.bfloat16),
             pltpu.VMEM((half_patches, 2 * rows, columns), jnp.bfloat16),
-            pltpu.SemaphoreType.DMA((2 + shots,)),
+            pltpu.SemaphoreType.DMA((6 + shots,)),
             pltpu.SemaphoreType.DMA((nfreq - 1,)),
             pltpu.SemaphoreType.DMA((nfreq - 1,)),
             pltpu.SemaphoreType.DMA((nfreq, group // 2 - 1)),

time: 19 us -> 18.3 us (0.963)
  Pallas kernels: 17.3 us -> 16.6 us
    pallas_call x1, Pallas kernels: 17.3 us -> 16.6 us  [on_device(): pl.pallas_call(functools.partial(kernel, nfs, nfreq, half_patches), out_s...]
where the time goes in v3:
time: 18.3 us; the launch traced here: 18.1 us
  Pallas kernels  16.6 us (91%)
  local copies, waits for them, and re-layouts  1.52 us (8%)
    pallas_call x1, Pallas kernels, on_device(): pl.pallas_call(functools.partial(kernel, nfs, nfreq, half_patches), out_s...  16.6 us
    unnamed x1, local copies, waits for them, and re-layouts  1.52 us

profile of v3, /device:TPU:1, one launch (start us, length us, event | category | flops | bytes accessed | tf_op | source)
XLA Modules:
  0.0 18.1 jit_solution(13202399109424424097)
XLA Ops:
  0.0 16.6 %shard_map.73 = bf16[256,128]{1,0:T(8,128)(2,1)} custom-call(s32[4]{0:T(128)} %freq_hbm.1, s32[1,8]{1,0:T(1,128)} %pattern_hbm.1, s32[1,8]{1,0:T(1,128)} %mask_hbm.1, s32[1,128]{1,0:T(1,128)} %bins_hbm.1, f32[64,4,128]{2,1,0:T(4,128)} %bitcast.7, bf16[4,512,1024]{2,1,0:T(8,128)(2,1)} %traces_hbm.1, bf16[64,256,128]{2,1,0:T(8,128)(2,1)} %bitcast.5), custom_call_target="tpu_custom_call" | custom-call | tf_op jit(solution)/shard_map/pallas_call | solution.py:293
  16.6 1.5 %copy.9 = bf16[128,2,128]{2,1,0:T(2,128)(2,1)} copy(bf16[128,2,128]{2,1,0:T(2,128)(2,1)} %bitcast.6) | data formatting | bytes 131072

commit v4 on v3

--- a/solution.py
+++ b/solution.py
@@ -157,10 +157,9 @@
         weights.append(obl[pattern_ref[patch_id, b]] * live)
     weights = jnp.concatenate(weights, axis=1)
 
-    spectra = jnp.zeros((nfreq * pair, channels), jnp.float32)
     for s in range(shots):
         get_traces[s].wait()
-        spectra += dot(table[:, s * samples : (s + 1) * samples], traces[s])
+    spectra = dot(table[...], traces[...].reshape(shots * samples, channels))
     for f in range(nfreq):
         scaled = spectra[f * pair : (f + 1) * pair] * weights[f : f + 1]
         staged[f] = jnp.concatenate([scaled[:, :half], scaled[:, half:]], axis=0).astype(

time: 18.3 us -> 18.2 us (level)
  no operation moved by 1% of the time
where the time goes in v4:
time: 18.2 us; the launch traced here: 18.1 us
  Pallas kernels  16.5 us (91%)
  local copies, waits for them, and re-layouts  1.52 us (8%)
    pallas_call x1, Pallas kernels, on_device(): pl.pallas_call(functools.partial(kernel, nfs, nfreq, half_patches), out_s...  16.5 us
    unnamed x1, local copies, waits for them, and re-layouts  1.52 us

profile of v4, /device:TPU:1, one launch (start us, length us, event | category | flops | bytes accessed | tf_op | source)
XLA Modules:
  0.0 18.1 jit_solution(11535171102667504623)
XLA Ops:
  0.0 16.5 %shard_map.73 = bf16[256,128]{1,0:T(8,128)(2,1)} custom-call(s32[4]{0:T(128)} %freq_hbm.1, s32[1,8]{1,0:T(1,128)} %pattern_hbm.1, s32[1,8]{1,0:T(1,128)} %mask_hbm.1, s32[1,128]{1,0:T(1,128)} %bins_hbm.1, f32[64,4,128]{2,1,0:T(4,128)} %bitcast.7, bf16[4,512,1024]{2,1,0:T(8,128)(2,1)} %traces_hbm.1, bf16[64,256,128]{2,1,0:T(8,128)(2,1)} %bitcast.5), custom_call_target="tpu_custom_call" | custom-call | tf_op jit(solution)/shard_map/pallas_call | solution.py:292
  16.5 1.5 %copy.9 = bf16[128,2,128]{2,1,0:T(2,128)(2,1)} copy(bf16[128,2,128]{2,1,0:T(2,128)(2,1)} %bitcast.6) | data formatting | bytes 131072
